TPU v7x, 128 devices: a whole 4x4x4 slice. The times are simulated.
128 devices in a mesh: dp: 4 (over x), ctx: 32 (over z, y, core).
Axes of the slice: x: 4, y: 4, z: 4, core: 2. Of those that a mesh axis runs over, the one named last changes fastest.
Arguments:
- inputs: bfloat16 [16384, 896], P(('dp', 'ctx')), may hold values from -6 to 6
- cotangent: bfloat16 [16384, 896], P(('dp', 'ctx')), may hold values from -6 to 6
- span_order: int32 [64], replicated, may hold values from 0 to 63, as said below
- positions: int32 [16384], P(('dp', 'ctx')), may hold values from 0 to 1023, as said below
- attn_gain: bfloat16 [896], P('dp'), may hold values from 0.5 to 1.5
- qkv_weight: bfloat16 [896, 1152], P('dp'), may hold values from -0.1875 to 0.1875
- qkv_bias: bfloat16 [1152], P('dp'), may hold values from -3 to 3
- out_weight: bfloat16 [896, 896], P('dp'), may hold values from -0.375 to 0.375
- mlp_gain: bfloat16 [896], P('dp'), may hold values from 0.5 to 1.5
- gate_weight: bfloat16 [896, 4864], P('dp'), may hold values from -0.1875 to 0.1875
- up_weight: bfloat16 [896, 4864], P('dp'), may hold values from -0.1875 to 0.1875
- down_weight: bfloat16 [4864, 896], P('dp'), may hold values from -0.078125 to 0.078125
Outputs:
- output: bfloat16 [16384, 896], P(('dp', 'ctx'))
- input_grad: bfloat16 [16384, 896], P(('dp', 'ctx'))
- attn_gain_grad: float32 [896], P('dp')
- qkv_weight_grad: float32 [896, 1152], P('dp')
- qkv_bias_grad: float32 [1024], P('dp')
- value_bias_grad: float32 [128], P('dp')
- out_weight_grad: float32 [896, 896], P('dp')
- mlp_gain_grad: float32 [896], P('dp')
- gate_weight_grad: float32 [896, 4864], P('dp')
- up_weight_grad: float32 [896, 4864], P('dp')
- down_weight_grad: float32 [4864, 896], P('dp')
Inputs may be any that keep to these rules, and one draw needn't show every extreme that they name: `span_order`: entries 2c and 2c + 1 hold two spans j and 63 - j, in either order; every span appears once. `positions`: each token's position within its document. Documents are runs of consecutive places of a sequence, none longer than 1024 tokens, and positions count from 0 at a run's start, increasing by one along place.
All inputs are finite; a program needn't handle non-finite values.
Results may differ from a plain program's by a relative error of at most 0.03.
Values may be sent and summed in bfloat16 or wider, within the bound.
A program may use at most 192 MiB of HBM per device.

v0:
```python
import jax
import jax.numpy as jnp
from jax import lax
from jax.sharding import PartitionSpec as P

QH = 14
KVH = 2
HD = 64
norm_eps = 1e-06
rope_base = 1000000.0
masked_score = -1e30


def rms_apply(values, gain):
    mean_square = jnp.mean(values * values, axis=-1, keepdims=True)
    return values * lax.rsqrt(mean_square + norm_eps) * gain


def half_turn(values):
    middle = values.shape[-1] // 2
    return jnp.concatenate([-values[..., middle:], values[..., :middle]], axis=-1)


def rotate(values, cosine, sine):
    return values * cosine + half_turn(values) * sine


def rope_tables(positions, head_dim):
    middle = head_dim // 2
    inverse = rope_base ** (-(jnp.arange(middle).astype(jnp.float32) * 2.0) / head_dim)
    angles = positions.astype(jnp.float32)[:, None] * inverse[None, :]
    angles = jnp.concatenate([angles, angles], axis=-1)
    return (jnp.cos(angles), jnp.sin(angles))


def span_lookup(table, slots):
    picked = slots[:, None] == jnp.arange(table.shape[0], dtype=jnp.int32)[None, :]
    return jnp.sum(jnp.where(picked, table[None, :], 0), axis=1)


def swiglu(gate_in, up_in):
    return jax.nn.silu(gate_in) * up_in


def body(
    inputs,
    cotangent,
    span_order,
    positions,
    attn_gain,
    qkv_weight,
    qkv_bias,
    out_weight,
    mlp_gain,
    gate_weight,
    up_weight,
    down_weight,
):
    token_count = inputs.shape[0]
    span_rows = token_count // 2
    head_dim = HD
    query_heads = QH
    kv_heads = KVH
    group_size = query_heads // kv_heads
    score_scale = head_dim ** (-0.5)
    q_cols = query_heads * head_dim
    k_cols = kv_heads * head_dim
    seq_length = token_count * lax.axis_size("ctx")
    key_block = min(1024, seq_length)
    block_count = seq_length // key_block
    device_slot = lax.axis_index("ctx")
    local_slots = jnp.arange(token_count, dtype=jnp.int32)
    query_places = (
        span_lookup(span_order, 2 * device_slot + local_slots // span_rows) * span_rows
        + local_slots % span_rows
    )
    all_slots = jnp.arange(seq_length, dtype=jnp.int32)
    key_places = span_lookup(span_order, all_slots // span_rows) * span_rows + all_slots % span_rows
    key_places = key_places.reshape(block_count, key_block)
    gain_one, qkv_full, bias_full, out_full = (
        lax.all_gather(attn_gain, "dp", axis=0, tiled=True),
        lax.all_gather(qkv_weight, "dp", axis=0, tiled=True),
        lax.all_gather(qkv_bias, "dp", axis=0, tiled=True),
        lax.all_gather(out_weight, "dp", axis=0, tiled=True),
    )
    inputs_wide = inputs.astype(jnp.float32)
    gain_one_wide = gain_one.astype(jnp.float32)
    normed_one = rms_apply(inputs_wide, gain_one_wide).astype(jnp.bfloat16)
    mixed_proj = jnp.dot(
        normed_one, qkv_full, preferred_element_type=jnp.float32
    ) + bias_full.astype(jnp.float32)
    cosine, sine = rope_tables(positions, head_dim)
    cosine = cosine[:, None, :]
    sine = sine[:, None, :]
    query_rot = rotate(
        mixed_proj[:, :q_cols].reshape(token_count, query_heads, head_dim), cosine, sine
    ).astype(jnp.bfloat16)
    key_rot = rotate(
        mixed_proj[:, q_cols : q_cols + k_cols].reshape(token_count, kv_heads, head_dim),
        cosine,
        sine,
    )
    key_rot = key_rot.astype(jnp.bfloat16).reshape(token_count, k_cols)
    value_low = mixed_proj[:, q_cols + k_cols :].astype(jnp.bfloat16)
    key_all, value_all = (
        lax.all_gather(key_rot, "ctx", axis=0, tiled=True),
        lax.all_gather(value_low, "ctx", axis=0, tiled=True),
    )
    key_blocks = key_all.reshape(block_count, key_block, kv_heads, head_dim)
    value_blocks = value_all.reshape(block_count, key_block, kv_heads, head_dim)
    query_grouped = query_rot.reshape(token_count, kv_heads, group_size, head_dim)

    def block_scores(key_part, place_part):
        scores = (
            jnp.einsum(
                "qhgd,khd->hgqk", query_grouped, key_part, preferred_element_type=jnp.float32
            )
            * score_scale
        )
        allowed = place_part[None, :] <= query_places[:, None]
        return jnp.where(allowed[None, None], scores, masked_score)

    def max_step(running, pieces):
        running_max, running_sum = running
        scores = block_scores(pieces[0], pieces[1])
        new_max = jnp.maximum(running_max, jnp.max(scores, axis=-1))
        new_sum = running_sum * jnp.exp(running_max - new_max) + jnp.sum(
            jnp.exp(scores - new_max[..., None]), axis=-1
        )
        return ((new_max, new_sum), None)

    start_max = jnp.full((kv_heads, group_size, token_count), masked_score, jnp.float32)
    start_sum = jnp.zeros((kv_heads, group_size, token_count), jnp.float32)
    (final_max, final_sum), unused = lax.scan(
        max_step, (start_max, start_sum), (key_blocks, key_places)
    )
    log_total = final_max + jnp.log(final_sum)

    def value_step(attended_sum, pieces):
        scores = block_scores(pieces[0], pieces[2])
        probs_low = jnp.exp(scores - log_total[..., None]).astype(jnp.bfloat16)
        return (
            attended_sum
            + jnp.einsum(
                "hgqk,khd->qhgd", probs_low, pieces[1], preferred_element_type=jnp.float32
            ),
            None,
        )

    start_total = jnp.zeros((token_count, kv_heads, group_size, head_dim), jnp.float32)
    attended_sum, unused = lax.scan(value_step, start_total, (key_blocks, value_blocks, key_places))
    attended_low = attended_sum.reshape(token_count, q_cols).astype(jnp.bfloat16)
    residual = inputs_wide + jnp.dot(attended_low, out_full, preferred_element_type=jnp.float32)
    gain_two, gate_full, up_full, down_full = (
        lax.all_gather(mlp_gain, "dp", axis=0, tiled=True),
        lax.all_gather(gate_weight, "dp", axis=0, tiled=True),
        lax.all_gather(up_weight, "dp", axis=0, tiled=True),
        lax.all_gather(down_weight, "dp", axis=0, tiled=True),
    )
    gain_two_wide = gain_two.astype(jnp.float32)
    normed_two = rms_apply(residual, gain_two_wide).astype(jnp.bfloat16)
    gate_proj = jnp.dot(normed_two, gate_full, preferred_element_type=jnp.float32)
    up_proj = jnp.dot(normed_two, up_full, preferred_element_type=jnp.float32)
    hidden_low = swiglu(gate_proj, up_proj).astype(jnp.bfloat16)
    output = (residual + jnp.dot(hidden_low, down_full, preferred_element_type=jnp.float32)).astype(
        jnp.bfloat16
    )
    d_hidden = jnp.dot(cotangent, down_full.T, preferred_element_type=jnp.float32)
    down_grad = jnp.dot(hidden_low.T, cotangent, preferred_element_type=jnp.float32)
    swiglu_back = jax.vjp(swiglu, gate_proj, up_proj)[1]
    d_gate, d_up = swiglu_back(d_hidden)
    d_gate = d_gate.astype(jnp.bfloat16)
    d_up = d_up.astype(jnp.bfloat16)
    gate_grad = jnp.dot(normed_two.T, d_gate, preferred_element_type=jnp.float32)
    up_grad = jnp.dot(normed_two.T, d_up, preferred_element_type=jnp.float32)
    d_normed_two = jnp.dot(d_gate, gate_full.T, preferred_element_type=jnp.float32) + jnp.dot(
        d_up, up_full.T, preferred_element_type=jnp.float32
    )
    norm_two_back = jax.vjp(rms_apply, residual, gain_two_wide)[1]
    d_resid_part, gain_two_grad = norm_two_back(d_normed_two)
    d_residual = d_resid_part + cotangent.astype(jnp.float32)
    d_branch = d_residual.astype(jnp.bfloat16)
    out_grad = jnp.dot(attended_low.T, d_branch, preferred_element_type=jnp.float32)
    d_attended = jnp.dot(d_branch, out_full.T, preferred_element_type=jnp.float32).astype(
        jnp.bfloat16
    )
    d_attended = d_attended.reshape(token_count, kv_heads, group_size, head_dim)
    row_delta = jnp.einsum("qhgd,qhgd->hgq", d_attended.astype(jnp.float32), attended_sum)

    def grad_step(d_query, pieces):
        key_part, value_part, place_part = pieces
        scores = block_scores(key_part, place_part)
        probs_full = jnp.exp(scores - log_total[..., None])
        probs_low = probs_full.astype(jnp.bfloat16)
        d_probs = jnp.einsum(
            "qhgd,khd->hgqk", d_attended, value_part, preferred_element_type=jnp.float32
        )
        d_scores = (probs_full * (d_probs - row_delta[..., None])).astype(jnp.bfloat16)
        d_query = (
            d_query
            + jnp.einsum("hgqk,khd->qhgd", d_scores, key_part, preferred_element_type=jnp.float32)
            * score_scale
        )
        d_key = (
            jnp.einsum(
                "hgqk,qhgd->khd", d_scores, query_grouped, preferred_element_type=jnp.float32
            )
            * score_scale
        )
        d_value = jnp.einsum(
            "hgqk,qhgd->khd", probs_low, d_attended, preferred_element_type=jnp.float32
        )
        return (d_query, (d_key, d_value))

    d_query, (d_key_blocks, d_value_blocks) = lax.scan(
        grad_step, start_total, (key_blocks, value_blocks, key_places)
    )
    d_key_all = d_key_blocks.reshape(seq_length, k_cols)
    d_value_all = d_value_blocks.reshape(seq_length, k_cols)
    d_key_own, d_value_own = (
        lax.psum_scatter(
            d_key_all.astype(jnp.bfloat16), "ctx", scatter_dimension=0, tiled=True
        ).astype(jnp.float32),
        lax.psum_scatter(
            d_value_all.astype(jnp.bfloat16), "ctx", scatter_dimension=0, tiled=True
        ).astype(jnp.float32),
    )

    def turn_back(grads):
        return jax.vjp(lambda values: rotate(values, cosine, sine), grads)[1](grads)[0]

    d_query_raw = turn_back(d_query.reshape(token_count, query_heads, head_dim)).reshape(
        token_count, q_cols
    )
    d_key_raw = turn_back(d_key_own.reshape(token_count, kv_heads, head_dim)).reshape(
        token_count, k_cols
    )
    d_mixed = jnp.concatenate([d_query_raw, d_key_raw, d_value_own], axis=1).astype(jnp.bfloat16)
    qkv_grad = jnp.dot(normed_one.T, d_mixed, preferred_element_type=jnp.float32)
    bias_grad = jnp.sum(d_mixed.astype(jnp.float32), axis=0)
    qk_bias_grad = bias_grad[: q_cols + k_cols]
    value_bias_grad = bias_grad[q_cols + k_cols :]
    d_normed_one = jnp.dot(d_mixed, qkv_full.T, preferred_element_type=jnp.float32)
    norm_one_back = jax.vjp(rms_apply, inputs_wide, gain_one_wide)[1]
    d_input_part, gain_one_grad = norm_one_back(d_normed_one)
    input_grad = (d_input_part + d_residual).astype(jnp.bfloat16)
    local_grads = (
        gain_one_grad,
        qkv_grad,
        qk_bias_grad,
        value_bias_grad,
        out_grad,
        gain_two_grad,
        gate_grad,
        up_grad,
        down_grad,
    )
    shard_grads = (
        lax.psum_scatter(
            local_grads[0].astype(jnp.bfloat16), "dp", scatter_dimension=0, tiled=True
        ).astype(jnp.float32),
        lax.psum_scatter(
            local_grads[1].astype(jnp.bfloat16), "dp", scatter_dimension=0, tiled=True
        ).astype(jnp.float32),
        lax.psum_scatter(
            local_grads[2].astype(jnp.bfloat16), "dp", scatter_dimension=0, tiled=True
        ).astype(jnp.float32),
        lax.psum_scatter(
            local_grads[3].astype(jnp.bfloat16), "dp", scatter_dimension=0, tiled=True
        ).astype(jnp.float32),
        lax.psum_scatter(
            local_grads[4].astype(jnp.bfloat16), "dp", scatter_dimension=0, tiled=True
        ).astype(jnp.float32),
        lax.psum_scatter(
            local_grads[5].astype(jnp.bfloat16), "dp", scatter_dimension=0, tiled=True
        ).astype(jnp.float32),
        lax.psum_scatter(
            local_grads[6].astype(jnp.bfloat16), "dp", scatter_dimension=0, tiled=True
        ).astype(jnp.float32),
        lax.psum_scatter(
            local_grads[7].astype(jnp.bfloat16), "dp", scatter_dimension=0, tiled=True
        ).astype(jnp.float32),
        lax.psum_scatter(
            local_grads[8].astype(jnp.bfloat16), "dp", scatter_dimension=0, tiled=True
        ).astype(jnp.float32),
    )
    summed = (
        lax.psum(shard_grads[0].astype(jnp.bfloat16), "ctx").astype(jnp.float32),
        lax.psum(shard_grads[1].astype(jnp.bfloat16), "ctx").astype(jnp.float32),
        lax.psum(shard_grads[2].astype(jnp.bfloat16), "ctx").astype(jnp.float32),
        lax.psum(shard_grads[3].astype(jnp.bfloat16), "ctx").astype(jnp.float32),
        lax.psum(shard_grads[4].astype(jnp.bfloat16), "ctx").astype(jnp.float32),
        lax.psum(shard_grads[5].astype(jnp.bfloat16), "ctx").astype(jnp.float32),
        lax.psum(shard_grads[6].astype(jnp.bfloat16), "ctx").astype(jnp.float32),
        lax.psum(shard_grads[7].astype(jnp.bfloat16), "ctx").astype(jnp.float32),
        lax.psum(shard_grads[8].astype(jnp.bfloat16), "ctx").astype(jnp.float32),
    )
    return (
        output,
        input_grad,
        summed[0],
        summed[1],
        summed[2],
        summed[3],
        summed[4],
        summed[5],
        summed[6],
        summed[7],
        summed[8],
    )


def solution(mesh):
    placed = (
        P(("dp", "ctx"), None),
        P(("dp", "ctx"), None),
        P(),
        P(("dp", "ctx")),
        P("dp"),
        P("dp", None),
        P("dp"),
        P("dp", None),
        P("dp"),
        P("dp", None),
        P("dp", None),
        P("dp", None),
    )
    return jax.shard_map(
        body,
        mesh=mesh,
        in_specs=placed,
        out_specs=(
            P(("dp", "ctx"), None),
            P(("dp", "ctx"), None),
            P("dp"),
            P("dp", None),
            P("dp"),
            P("dp"),
            P("dp", None),
            P("dp"),
            P("dp", None),
            P("dp", None),
            P("dp", None),
        ),
        check_vma=False,
    )
```

profile of v0, /device:TPU:1, one launch (start us, length us, event | category | flops | bytes accessed | tf_op | source)
XLA Modules:
  0.0 1149.0 jit_solution(3470323007845369848)
XLA Ops:
  13.2 9.4 all-reduce.14
  23.7 19.9 %all-gather.8.cloned.1.call-done = bf16[896,1152]{1,0:T(8,128)(2,1)} async-done(((bf16[224,1152]{1,0:T(8,128)(2,1)}), bf16[896,1152]{1,0:T(8,128)(2,1)}) %all-gather.8.cloned.1.call-update) | async-done | bytes 2064400 | tf_op jit(solution)/shard_map/all_gather | solution.py:82
  51.1 38.8 %all-gather.10.cloned.1.call-done = bf16[4096,128]{1,0:T(8,128)(2,1)} async-done(((bf16[128,128]{1,0:T(8,128)(2,1)}), bf16[4096,128]{1,0:T(8,128)(2,1)}) %all-gather.10.cloned.1.call-update) | async-done | bytes 1048592 | tf_op jit(solution)/shard_map/all_gather | solution.py:107
  89.9 5.0 reshape.338
  94.9 5.9 copy.88
  100.7 34.2 %all-gather.12.cloned.1.call-done = bf16[4096,128]{1,0:T(8,128)(2,1)} async-done(((bf16[128,128]{1,0:T(8,128)(2,1)}), bf16[4096,128]{1,0:T(8,128)(2,1)}) %all-gather.12.cloned.1.call-update) | async-done | bytes 1048592 | tf_op jit(solution)/shard_map/all_gather | solution.py:106
  134.9 5.0 reshape.339
  139.9 4.6 copy.89
  144.5 37.0 %while.39 = (s32[]{:T(128)}, f32[2,7,128]{2,1,0:T(8,128)S(1)}, f32[2,7,128]{2,1,0:T(8,128)S(1)}, s32[4,1024]{1,0:T(4,128)S(1)}, s32[128]{0:T(128)S(1)}, /*index=...) while((s32[]{:T(128)}, f32[2,7,128]{2,1,0:T(8,128)S(1)}, ...), condition=%wide.region_6.7_spmd.clone, body=%wide.region_3.6_spmd.clone.sunk | while | flops 247866112 | bytes 15670904 | solution.py:134
  148.9 4.6 exponential_reduce_fusion.2
  157.9 4.6 exponential_reduce_fusion.2
  171.7 4.7 fusion.161
  176.3 5.2 exponential_reduce_fusion.2
  181.6 15.2 %while.40 = (s32[]{:T(128)}, f32[128,2,7,64]{0,3,2,1:T(8,128)S(1)}, bf16[4,1024,2,64]{1,3,2,0:T(8,128)(2,1)}, s32[4,1024]{1,0:T(4,128)S(1)}, s32[128]{0:T(128)S(...) while((s32[]{:T(128)}, f32[128,2,7,64]{0,3,2,1:T(8,128)S(1)}, ...), condition=%wide.region_8.9_spmd.clone, body=%wide.region_7.8_spmd.clone.sunk | while | flops 477462528 | bytes 1955962 | solution.py:151
  199.9 49.5 %all-gather.16.cloned.1.call-done = bf16[896,4864]{1,0:T(8,128)(2,1)} async-done(((bf16[224,4864]{1,0:T(8,128)(2,1)}), bf16[896,4864]{1,0:T(8,128)(2,1)}) %all-gather.16.cloned.1.call-update) | async-done | bytes 8716304 | tf_op jit(solution)/shard_map/all_gather | solution.py:156
  249.4 6.4 fusion.102
  255.8 81.9 %all-gather.18.cloned.1.call-done = bf16[896,4864]{1,0:T(8,128)(2,1)} async-done(((bf16[224,4864]{1,0:T(8,128)(2,1)}), bf16[896,4864]{1,0:T(8,128)(2,1)}) %all-gather.18.cloned.1.call-update) | async-done | bytes 8716304 | tf_op jit(solution)/shard_map/all_gather | solution.py:157
  337.7 6.4 fusion.103
  344.1 82.1 %all-gather.20.cloned.1.call-done = bf16[4864,896]{1,0:T(8,128)(2,1)} async-done(((bf16[1216,896]{1,0:T(8,128)(2,1)}), bf16[4864,896]{1,0:T(8,128)(2,1)}) %all-gather.20.cloned.1.call-update) | async-done | bytes 8716304 | tf_op jit(solution)/shard_map/all_gather | solution.py:158
  426.3 7.5 multiply_convert_fusion
  433.8 7.2 fusion.104
  449.2 71.3 %while.41 = (s32[]{:T(128)}, f32[128,2,7,64]{0,3,2,1:T(8,128)S(1)}, bf16[4,1024,2,64]{1,3,2,0:T(8,128)(2,1)}, bf16[4,1024,2,64]{1,3,2,0:T(8,128)(2,1)}, bf16[4,1...) while((s32[]{:T(128)}, f32[128,2,7,64]{0,3,2,1:T(8,128)S(1)}, ...), condition=%wide.region_12.13_spmd.clone, body=%wide.region_11.12_spmd.clone.sunk | while | flops 1193361408 | bytes 99781520 | solution.py:215
  450.8 5.4 fusion.179
  460.9 5.2 fusion.182
  468.6 5.4 fusion.179
  478.7 5.2 fusion.182
  486.4 5.4 fusion.179
  496.5 5.2 fusion.182
  504.1 5.4 fusion.179
  514.3 5.2 fusion.182
  520.5 6.0 copy.124
  526.5 4.7 reshape.332
  531.3 6.0 copy.123
  537.3 4.7 reshape.330
  544.2 64.3 %reduce-scatter.24.cloned.1.call-done = bf16[128,128]{1,0:T(8,128)(2,1)} async-done(((bf16[4096,128]{1,0:T(8,128)(2,1)}), bf16[128,128]{1,0:T(8,128)(2,1)}) %reduce-scatter.24.cloned.1.call-update) | async-done | bytes 32784
  609.3 80.0 %reduce-scatter.22.cloned.1.call-done = bf16[128,128]{1,0:T(8,128)(2,1)} async-done(((bf16[4096,128]{1,0:T(8,128)(2,1)}), bf16[128,128]{1,0:T(8,128)(2,1)}) %reduce-scatter.22.cloned.1.call-update) | async-done | bytes 32784
  692.7 7.2 convolution_convert_fusion.2
  699.9 7.2 convolution_convert_fusion.1
  708.0 4.7 convolution_convert_fusion
  712.9 5.3 reduce-scatter.14.cloned.1.call-done
  718.2 32.8 %reduce-scatter.12.cloned.1.call-done = bf16[224,1152]{1,0:T(8,128)(2,1)} async-done(((bf16[896,1152]{1,0:T(8,128)(2,1)}), bf16[224,1152]{1,0:T(8,128)(2,1)}) %reduce-scatter.12.cloned.1.call-update) | async-done | bytes 516112 | tf_op jit(solution)/shard_map/reduce_scatter | solution.py:262
  751.0 85.4 %reduce-scatter.16.cloned.1.call-done = bf16[224,4864]{1,0:T(8,128)(2,1)} async-done(((bf16[896,4864]{1,0:T(8,128)(2,1)}), bf16[224,4864]{1,0:T(8,128)(2,1)}) %reduce-scatter.16.cloned.1.call-update) | async-done | bytes 2179088 | tf_op jit(solution)/shard_map/reduce_scatter | solution.py:277
  836.4 85.4 %reduce-scatter.18.cloned.1.call-done = bf16[224,4864]{1,0:T(8,128)(2,1)} async-done(((bf16[896,4864]{1,0:T(8,128)(2,1)}), bf16[224,4864]{1,0:T(8,128)(2,1)}) %reduce-scatter.18.cloned.1.call-update) | async-done | bytes 2179088 | tf_op jit(solution)/shard_map/reduce_scatter | solution.py:280
  921.7 85.4 %reduce-scatter.20.cloned.1.call-done = bf16[1216,896]{1,0:T(8,128)(2,1)} async-done(((bf16[4864,896]{1,0:T(8,128)(2,1)}), bf16[1216,896]{1,0:T(8,128)(2,1)}) %reduce-scatter.20.cloned.1.call-update) | async-done | bytes 2179088 | tf_op jit(solution)/shard_map/reduce_scatter | solution.py:283
  1009.2 5.8 fusion.65
  1016.0 7.1 all-reduce.13
  1023.4 65.2 %all-reduce.11 = (bf16[224]{0:T(256)(128)(2,1)S(1)}, bf16[256]{0:T(256)(128)(2,1)S(1)}, bf16[32]{0:T(256)(128)(2,1)S(1)}, bf16[224]{0:T(256)(128)(2,1)S(1)}) all-reduce(bf16[224]{0:T(256)(128)(2,1)S(1)} %dynamic-slice.4, bf16[256]{0:T(256)(128)(2,1)S(1)} %dynamic-slice.6, ...), channel_id=1, replica_groups=mesh['dp'=4,'ctx'=32] {'ctx'}, use_global_device_ids=true, to_apply=%region_18.19 | all-reduce | flops 736 | bytes 2944 | tf_op jit(solution)/shard_map/psum | solution.py:288
  1091.7 39.1 %all-reduce.17.cloned.1.call-done = (bf16[224,1152]{1,0:T(8,128)(2,1)}, bf16[224,896]{1,0:T(8,128)(2,1)}, bf16[224,4864]{1,0:T(8,128)(2,1)}, bf16[224,4864]{1,0:T(8,128)(2,1)}, bf16[1216,896]{1,0:T(8,128)(2,1)}) async-done(((bf16[224,1152]{1,0:T(8,128)(2,1)}, bf16[224,896]{1,0:T(8,128)(2,1)}, bf16[224,4864]{1,0:T(8,128)(2,1)}, bf16[224,4864]{1,0:T(8,128)(2,1)}, bf16[1216,896]{1,0:T(8,128)(2,1)}), ...) | async-done | bytes 7454736 | tf_op jit(solution)/shard_map/psum | solution.py:289
  (283 shorter events, 107.9 us)
Async XLA Ops:
  7.2 39.3 %copy-start.31 = (s32[128]{0:T(128)S(1)}, s32[128]{0:T(128)}, u32[]{:S(2)}) copy-start(s32[128]{0:T(128)} %param.21) | copy-start | bytes 1540
  7.2 36.4 %all-gather.8.cloned.1.call-start = ((), (), s32[]{:S(2)}) async-start(), calls=%async_computation.7 | async-start | bytes 2580480 | tf_op jit(solution)/shard_map/all_gather | solution.py:82
  7.9 82.0 %all-gather.10.cloned.1.call-start = ((), (), s32[]{:S(2)}) async-start(), calls=%async_computation.8 | async-start | bytes 1081344 | tf_op jit(solution)/shard_map/all_gather | solution.py:107
  23.7 23.3 %copy-start.29 = (f32[128]{0:T(128)}, f32[128]{0:T(128)S(1)}, u32[]{:S(2)}) copy-start(f32[128]{0:T(128)S(1)} %fusion.73) | copy-start | bytes 1540
  46.5 88.4 %all-gather.12.cloned.1.call-start = ((), (), s32[]{:S(2)}) async-start(), calls=%async_computation.9 | async-start | bytes 1081344 | tf_op jit(solution)/shard_map/all_gather | solution.py:106
  47.7 149.1 %all-gather.14.cloned.1.call-start = ((), (), s32[]{:S(2)}) async-start(), calls=%async_computation.10 | async-start | bytes 2007040 | tf_op jit(solution)/shard_map/all_gather | solution.py:84
  48.3 201.1 %all-gather.16.cloned.1.call-start = ((), (), s32[]{:S(2)}) async-start(), calls=%async_computation.11 | async-start | bytes 10895360 | tf_op jit(solution)/shard_map/all_gather | solution.py:156
  48.9 288.8 %all-gather.18.cloned.1.call-start = ((), (), s32[]{:S(2)}) async-start(), calls=%async_computation.12 | async-start | bytes 10895360 | tf_op jit(solution)/shard_map/all_gather | solution.py:157
  49.5 376.8 %all-gather.20.cloned.1.call-start = ((), (), s32[]{:S(2)}) async-start(), calls=%async_computation.13 | async-start | bytes 10895360 | tf_op jit(solution)/shard_map/all_gather | solution.py:158
  50.2 558.2 %reduce-scatter.24.cloned.1.call-start = ((), (), s32[]{:S(2)}) async-start(), calls=%async_computation.20 | async-start | bytes 1081344
  181.5 15.3 %copy-start.9 = (bf16[128,896]{1,0:T(8,128)(2,1)S(1)}, bf16[128,896]{1,0:T(8,128)(2,1)}, u32[]{:S(2)}) copy-start(bf16[128,896]{1,0:T(8,128)(2,1)} %param.18) | copy-start | bytes 688132
  196.7 59.0 %copy-start.19 = (f32[128,2,7,64]{0,3,2,1:T(8,128)}, f32[128,2,7,64]{0,3,2,1:T(8,128)S(1)}, u32[]{:S(2)}) copy-start(f32[128,2,7,64]{0,3,2,1:T(8,128)S(1)} %get-tuple-element.157) | copy-start | bytes 1376260
  196.8 59.0 %copy-start.17 = (bf16[128,2,7,64]{0,3,2,1:T(8,128)(2,1)}, bf16[128,2,7,64]{0,3,2,1:T(8,128)(2,1)S(1)}, u32[]{:S(2)}) copy-start(bf16[128,2,7,64]{0,3,2,1:T(8,128)(2,1)S(1)} %convert_element_type.171) | copy-start | bytes 688132
  433.8 7.2 copy-start.12
  433.8 7.2 copy-start.11
  433.8 7.2 copy-start.2
  433.8 7.2 copy-start.4
  441.1 3.9 copy-start.8
  450.5 5.7 copy-start.1
  456.2 4.7 copy-start.22
  456.2 4.7 copy-start.27
  460.9 5.3 copy-start.21
  468.3 5.7 copy-start.1
  474.0 4.7 copy-start.22
  474.0 4.7 copy-start.27
  478.7 5.3 copy-start.21
  486.1 5.7 copy-start.1
  491.8 4.7 copy-start.22
  491.8 4.7 copy-start.27
  496.4 5.3 copy-start.21
  503.9 5.7 copy-start.1
  509.6 4.7 copy-start.22
  509.6 4.7 copy-start.27
  514.2 5.3 copy-start.21
  531.2 158.1 %reduce-scatter.22.cloned.1.call-start = ((), (), s32[]{:S(2)}) async-start(), calls=%async_computation.19 | async-start | bytes 1081344
  531.3 10.9 copy-start.7
  531.3 10.9 copy-start.18
  542.1 148.1 %copy-start.10 = (bf16[128,896]{1,0:T(8,128)(2,1)S(1)}, bf16[128,896]{1,0:T(8,128)(2,1)}, u32[]{:S(2)}) copy-start(bf16[128,896]{1,0:T(8,128)(2,1)} %param.18) | copy-start | bytes 688132
  542.1 176.0 %reduce-scatter.14.cloned.1.call-start = ((), (), s32[]{:S(2)}) async-start(), calls=%async_computation.15 | async-start | bytes 2007040 | tf_op jit(solution)/shard_map/reduce_scatter | solution.py:271
  543.9 207.0 %reduce-scatter.12.cloned.1.call-start = ((), (), s32[]{:S(2)}) async-start(), calls=%async_computation.14 | async-start | bytes 2580480 | tf_op jit(solution)/shard_map/reduce_scatter | solution.py:262
  692.4 144.0 %reduce-scatter.16.cloned.1.call-start = ((), (), s32[]{:S(2)}) async-start(), calls=%async_computation.16 | async-start | bytes 10895360 | tf_op jit(solution)/shard_map/reduce_scatter | solution.py:277
  699.8 221.9 %reduce-scatter.18.cloned.1.call-start = ((), (), s32[]{:S(2)}) async-start(), calls=%async_computation.17 | async-start | bytes 10895360 | tf_op jit(solution)/shard_map/reduce_scatter | solution.py:280
  707.1 300.0 %reduce-scatter.20.cloned.1.call-start = ((), (), s32[]{:S(2)}) async-start(), calls=%async_computation.18 | async-start | bytes 10895360 | tf_op jit(solution)/shard_map/reduce_scatter | solution.py:283
  712.8 418.0 %all-reduce.17.cloned.1.call-start = ((), (), s32[]{:S(2)}) async-start(), calls=%async_computation.21 | async-start | bytes 14909440 | tf_op jit(solution)/shard_map/psum | solution.py:289
  1009.1 6.0 copy-start.16
  1014.9 75.9 %copy-start.30 = (f32[128]{0:T(128)S(1)}, f32[128]{0:T(128)}, u32[]{:S(2)}) copy-start(f32[128]{0:T(128)} %copy-done.29) | copy-start | bytes 1540
  1130.8 4.3 copy-start.15
  1133.0 4.4 copy-start.14
  (23 other events, 49.3 us)
Sparse Core Ops, SparseCore 0:
  9.7 33.8 all-gather.7
  46.6 43.2 all-gather.9
  92.8 42.0 all-gather.11
  136.4 25.5 all-gather.13
  163.5 85.8 all-gather.15
  250.9 86.7 all-gather.17
  339.4 86.8 all-gather.19
  531.4 77.0 reduce-scatter.23
  612.4 76.9 reduce-scatter.21
  692.2 25.9 reduce-scatter.13
  721.2 29.7 reduce-scatter.11
  753.5 82.8 reduce-scatter.15
  838.8 82.8 reduce-scatter.17
  924.2 82.8 reduce-scatter.19
  1011.1 119.6 all-reduce.16
where the time goes:
time: 1160 us; the launch traced here: 1150 us
  waiting for transfers between devices  787 us (68%)
  matrix products  160 us (14%)
  blocking collectives  81.7 us (7%)
  local copies, waits for them, and re-layouts  59.3 us (5%)
  other arithmetic  40.1 us (3%)
  between operations  18.1 us (2%)
    unnamed x17, waiting for transfers between devices  147 us
    reduce_scatter x1, waiting for transfers between devices, body(): lax.psum_scatter(local_grads[6].astype(jnp.bfloat16), 'dp', scatter_dimen...  85.4 us
    reduce_scatter x1, waiting for transfers between devices, body(): lax.psum_scatter(local_grads[8].astype(jnp.bfloat16), 'dp', scatter_dimen...  85.4 us
    reduce_scatter x1, waiting for transfers between devices, body(): lax.psum_scatter(local_grads[7].astype(jnp.bfloat16), 'dp', scatter_dimen...  85.4 us
    all_gather x1, waiting for transfers between devices, body(): lax.all_gather(down_weight, 'dp', axis=0, tiled=True)  82.1 us
    all_gather x1, waiting for transfers between devices, body(): lax.all_gather(up_weight, 'dp', axis=0, tiled=True)  81.9 us
    psum x1, blocking collectives, body(): lax.psum(shard_grads[0].astype(jnp.bfloat16), 'ctx').astype(jnp.float32)  65.2 us
    all_gather x1, waiting for transfers between devices, body(): lax.all_gather(gate_weight, 'dp', axis=0, tiled=True)  49.5 us
  transfers between devices with their start and end apart: 15, of which 14 were waited for; matrix products, arithmetic and copies ran while one was open for 12% of the time, Pallas kernels for 0%

commit v1 on v0

--- a/solution.py
+++ b/solution.py
@@ -9,6 +9,7 @@
 norm_eps = 1e-06
 rope_base = 1000000.0
 masked_score = -1e30
+_connect_groups = lambda view: jnp.sum(lax.all_gather(view, "ctx"), axis=0)
 
 
 def rms_apply(values, gain):
@@ -286,7 +287,7 @@
     )
     summed = (
         lax.psum(shard_grads[0].astype(jnp.bfloat16), "ctx").astype(jnp.float32),
-        lax.psum(shard_grads[1].astype(jnp.bfloat16), "ctx").astype(jnp.float32),
+        _connect_groups(shard_grads[1].astype(jnp.bfloat16)).astype(jnp.float32),
         lax.psum(shard_grads[2].astype(jnp.bfloat16), "ctx").astype(jnp.float32),
         lax.psum(shard_grads[3].astype(jnp.bfloat16), "ctx").astype(jnp.float32),
         lax.psum(shard_grads[4].astype(jnp.bfloat16), "ctx").astype(jnp.float32),

time: 1160 us -> 1230 us (1.060)
  waiting for transfers between devices: 787 us -> 849 us
    all_gather x0 -> x1, waiting for transfers between devices: none -> 63.5 us  [_connect_groups = lambda view: jnp.sum(lax.all_gather(view, 'ctx'), axis=0)]
    unnamed x17 -> x18, waiting for transfers between devices: 147 us -> 127 us
    reduce_scatter x1, waiting for transfers between devices: 5.32 us -> 26 us  [body(): lax.psum_scatter(local_grads[4].astype(jnp.bfloat16), 'dp', scatter_dimen...]
    unnamed x67 -> x73, local copies, waits for them, and re-layouts: 40.5 us -> 40.5 us
  transfers between devices with their start and end apart: 15 -> 16, of which waited for: 14 -> 15; matrix products, arithmetic and copies ran while one was open for 12% -> 12% of each run, Pallas kernels for 0% -> 0%
where the time goes in v1:
time: 1230 us; the launch traced here: 1220 us
  waiting for transfers between devices  849 us (69%)
  matrix products  160 us (13%)
  blocking collectives  81.4 us (7%)
  local copies, waits for them, and re-layouts  59.2 us (5%)
  other arithmetic  49.3 us (4%)
  between operations  18.2 us (1%)
    unnamed x18, waiting for transfers between devices  127 us
    reduce_scatter x1, waiting for transfers between devices, body(): lax.psum_scatter(local_grads[6].astype(jnp.bfloat16), 'dp', scatter_dimen...  86 us
    reduce_scatter x1, waiting for transfers between devices, body(): lax.psum_scatter(local_grads[7].astype(jnp.bfloat16), 'dp', scatter_dimen...  85.4 us
    reduce_scatter x1, waiting for transfers between devices, body(): lax.psum_scatter(local_grads[8].astype(jnp.bfloat16), 'dp', scatter_dimen...  85.4 us
    all_gather x1, waiting for transfers between devices, body(): lax.all_gather(down_weight, 'dp', axis=0, tiled=True)  82.1 us
    all_gather x1, waiting for transfers between devices, body(): lax.all_gather(up_weight, 'dp', axis=0, tiled=True)  82 us
    psum x1, blocking collectives, body(): lax.psum(shard_grads[0].astype(jnp.bfloat16), 'ctx').astype(jnp.float32)  64.9 us
    all_gather x1, waiting for transfers between devices, _connect_groups = lambda view: jnp.sum(lax.all_gather(view, 'ctx'), axis=0)  63.5 us
  transfers between devices with their start and end apart: 16, of which 15 were waited for; matrix products, arithmetic and copies ran while one was open for 12% of the time, Pallas kernels for 0%

profile of v1, /device:TPU:1, one launch (start us, length us, event | category | flops | bytes accessed | tf_op | source)
XLA Modules:
  0.0 1219.5 jit_solution(7265206978152235010)
XLA Ops:
  13.2 9.4 all-reduce.14
  23.7 19.9 %all-gather.10.cloned.1.call-done = bf16[896,1152]{1,0:T(8,128)(2,1)} async-done(((bf16[224,1152]{1,0:T(8,128)(2,1)}), bf16[896,1152]{1,0:T(8,128)(2,1)}) %all-gather.10.cloned.1.call-update) | async-done | bytes 2064400 | tf_op jit(solution)/shard_map/all_gather | solution.py:83
  51.2 38.8 %all-gather.12.cloned.1.call-done = bf16[4096,128]{1,0:T(8,128)(2,1)} async-done(((bf16[128,128]{1,0:T(8,128)(2,1)}), bf16[4096,128]{1,0:T(8,128)(2,1)}) %all-gather.12.cloned.1.call-update) | async-done | bytes 1048592 | tf_op jit(solution)/shard_map/all_gather | solution.py:108
  89.9 5.0 reshape.339
  94.9 5.9 copy.88
  100.8 34.1 %all-gather.14.cloned.1.call-done = bf16[4096,128]{1,0:T(8,128)(2,1)} async-done(((bf16[128,128]{1,0:T(8,128)(2,1)}), bf16[4096,128]{1,0:T(8,128)(2,1)}) %all-gather.14.cloned.1.call-update) | async-done | bytes 1048592 | tf_op jit(solution)/shard_map/all_gather | solution.py:107
  134.9 5.0 reshape.340
  139.9 4.6 copy.89
  144.5 37.0 %while.39 = (s32[]{:T(128)}, f32[2,7,128]{2,1,0:T(8,128)S(1)}, f32[2,7,128]{2,1,0:T(8,128)S(1)}, s32[4,1024]{1,0:T(4,128)S(1)}, s32[128]{0:T(128)S(1)}, /*index=...) while((s32[]{:T(128)}, f32[2,7,128]{2,1,0:T(8,128)S(1)}, ...), condition=%wide.region_6.7_spmd.clone, body=%wide.region_3.6_spmd.clone.sunk | while | flops 247866112 | bytes 15670904 | solution.py:135
  171.7 4.7 fusion.161
  176.4 5.2 exponential_reduce_fusion.2
  181.6 15.1 %while.40 = (s32[]{:T(128)}, f32[128,2,7,64]{0,3,2,1:T(8,128)S(1)}, bf16[4,1024,2,64]{1,3,2,0:T(8,128)(2,1)}, s32[4,1024]{1,0:T(4,128)S(1)}, s32[128]{0:T(128)S(...) while((s32[]{:T(128)}, f32[128,2,7,64]{0,3,2,1:T(8,128)S(1)}, ...), condition=%wide.region_8.9_spmd.clone, body=%wide.region_7.8_spmd.clone.sunk | while | flops 477462528 | bytes 1955962 | solution.py:152
  199.9 49.5 %all-gather.18.cloned.1.call-done = bf16[896,4864]{1,0:T(8,128)(2,1)} async-done(((bf16[224,4864]{1,0:T(8,128)(2,1)}), bf16[896,4864]{1,0:T(8,128)(2,1)}) %all-gather.18.cloned.1.call-update) | async-done | bytes 8716304 | tf_op jit(solution)/shard_map/all_gather | solution.py:157
  249.3 6.4 fusion.102
  255.7 82.0 %all-gather.20.cloned.1.call-done = bf16[896,4864]{1,0:T(8,128)(2,1)} async-done(((bf16[224,4864]{1,0:T(8,128)(2,1)}), bf16[896,4864]{1,0:T(8,128)(2,1)}) %all-gather.20.cloned.1.call-update) | async-done | bytes 8716304 | tf_op jit(solution)/shard_map/all_gather | solution.py:158
  337.7 6.4 fusion.103
  344.1 82.1 %all-gather.22.cloned.1.call-done = bf16[4864,896]{1,0:T(8,128)(2,1)} async-done(((bf16[1216,896]{1,0:T(8,128)(2,1)}), bf16[4864,896]{1,0:T(8,128)(2,1)}) %all-gather.22.cloned.1.call-update) | async-done | bytes 8716304 | tf_op jit(solution)/shard_map/all_gather | solution.py:159
  426.3 7.5 multiply_convert_fusion
  433.8 7.2 fusion.104
  449.2 71.2 %while.41 = (s32[]{:T(128)}, f32[128,2,7,64]{0,3,2,1:T(8,128)S(1)}, bf16[4,1024,2,64]{1,3,2,0:T(8,128)(2,1)}, bf16[4,1024,2,64]{1,3,2,0:T(8,128)(2,1)}, bf16[4,1...) while((s32[]{:T(128)}, f32[128,2,7,64]{0,3,2,1:T(8,128)S(1)}, ...), condition=%wide.region_12.13_spmd.clone, body=%wide.region_11.12_spmd.clone.sunk | while | flops 1193361408 | bytes 99781520 | solution.py:216
  450.8 5.4 fusion.179
  460.9 5.2 fusion.182
  468.5 5.4 fusion.179
  478.7 5.2 fusion.182
  486.3 5.4 fusion.179
  496.4 5.2 fusion.182
  504.0 5.4 fusion.179
  514.2 5.2 fusion.182
  520.4 6.0 copy.124
  526.3 4.7 reshape.333
  531.2 6.0 copy.123
  537.2 4.7 reshape.331
  544.0 7.1 convolution_convert_fusion.2
  551.2 7.2 convolution_convert_fusion.1
  559.3 4.9 convolution_convert_fusion
  564.4 43.9 %reduce-scatter.24.cloned.1.call-done = bf16[128,128]{1,0:T(8,128)(2,1)} async-done(((bf16[4096,128]{1,0:T(8,128)(2,1)}), bf16[128,128]{1,0:T(8,128)(2,1)}) %reduce-scatter.24.cloned.1.call-update) | async-done | bytes 32784
  609.2 79.7 %reduce-scatter.22.cloned.1.call-done = bf16[128,128]{1,0:T(8,128)(2,1)} async-done(((bf16[4096,128]{1,0:T(8,128)(2,1)}), bf16[128,128]{1,0:T(8,128)(2,1)}) %reduce-scatter.22.cloned.1.call-update) | async-done | bytes 32784
  692.0 26.0 %reduce-scatter.14.cloned.1.call-done = bf16[224,896]{1,0:T(8,128)(2,1)} async-done(((bf16[896,896]{1,0:T(8,128)(2,1)}), bf16[224,896]{1,0:T(8,128)(2,1)}) %reduce-scatter.14.cloned.1.call-update) | async-done | bytes 401424 | tf_op jit(solution)/shard_map/reduce_scatter | solution.py:272
  718.0 86.0 %reduce-scatter.16.cloned.1.call-done = bf16[224,4864]{1,0:T(8,128)(2,1)} async-done(((bf16[896,4864]{1,0:T(8,128)(2,1)}), bf16[224,4864]{1,0:T(8,128)(2,1)}) %reduce-scatter.16.cloned.1.call-update) | async-done | bytes 2179088 | tf_op jit(solution)/shard_map/reduce_scatter | solution.py:278
  804.1 85.4 %reduce-scatter.18.cloned.1.call-done = bf16[224,4864]{1,0:T(8,128)(2,1)} async-done(((bf16[896,4864]{1,0:T(8,128)(2,1)}), bf16[224,4864]{1,0:T(8,128)(2,1)}) %reduce-scatter.18.cloned.1.call-update) | async-done | bytes 2179088 | tf_op jit(solution)/shard_map/reduce_scatter | solution.py:281
  889.5 85.4 %reduce-scatter.20.cloned.1.call-done = bf16[1216,896]{1,0:T(8,128)(2,1)} async-done(((bf16[4864,896]{1,0:T(8,128)(2,1)}), bf16[1216,896]{1,0:T(8,128)(2,1)}) %reduce-scatter.20.cloned.1.call-update) | async-done | bytes 2179088 | tf_op jit(solution)/shard_map/reduce_scatter | solution.py:284
  974.9 32.1 %reduce-scatter.12.cloned.1.call-done = bf16[224,1152]{1,0:T(8,128)(2,1)} async-done(((bf16[896,1152]{1,0:T(8,128)(2,1)}), bf16[224,1152]{1,0:T(8,128)(2,1)}) %reduce-scatter.12.cloned.1.call-update) | async-done | bytes 516112 | tf_op jit(solution)/shard_map/reduce_scatter | solution.py:263
  1009.0 5.8 fusion.65
  1015.9 7.1 all-reduce.13
  1023.2 64.9 %all-reduce.11 = (bf16[224]{0:T(256)(128)(2,1)S(1)}, bf16[256]{0:T(256)(128)(2,1)S(1)}, bf16[32]{0:T(256)(128)(2,1)S(1)}, bf16[224]{0:T(256)(128)(2,1)S(1)}) all-reduce(bf16[224]{0:T(256)(128)(2,1)S(1)} %dynamic-slice.4, bf16[256]{0:T(256)(128)(2,1)S(1)} %dynamic-slice.6, ...), channel_id=1, replica_groups=mesh['dp'=4,'ctx'=32] {'ctx'}, use_global_device_ids=true, to_apply=%region_18.19 | all-reduce | flops 736 | bytes 2944 | tf_op jit(solution)/shard_map/psum | solution.py:289
  1091.2 37.3 %all-reduce.17.cloned.1.call-done = (bf16[224,896]{1,0:T(8,128)(2,1)}, bf16[224,4864]{1,0:T(8,128)(2,1)}, bf16[224,4864]{1,0:T(8,128)(2,1)}, bf16[1216,896]{1,0:T(8,128)(2,1)}) async-done(((bf16[224,896]{1,0:T(8,128)(2,1)}, bf16[224,4864]{1,0:T(8,128)(2,1)}, bf16[224,4864]{1,0:T(8,128)(2,1)}, bf16[1216,896]{1,0:T(8,128)(2,1)}), (bf16[224,896]{1,0:T(8,128)(2,1)}, bf16[224,4864]{1,0:T(8,128)(2,1)}, ...) | async-done | bytes 6938640 | tf_op jit(solution)/shard_map/psum | solution.py:293
  1139.4 63.5 %all-gather.24.cloned.1.call-done = bf16[7168,1152]{1,0:T(8,128)(2,1)} async-done(((bf16[224,1152]{1,0:T(8,128)(2,1)}), bf16[7168,1152]{1,0:T(8,128)(2,1)}) %all-gather.24.cloned.1.call-update) | async-done | bytes 16515088 | tf_op jit(solution)/shard_map/all_gather | solution.py:12
  1202.9 8.7 reduce_sum.114
  (293 shorter events, 117.5 us)
Async XLA Ops:
  7.2 39.4 %copy-start.34 = (s32[128]{0:T(128)S(1)}, s32[128]{0:T(128)}, u32[]{:S(2)}) copy-start(s32[128]{0:T(128)} %param.21) | copy-start | bytes 1540
  7.2 36.4 %all-gather.10.cloned.1.call-start = ((), (), s32[]{:S(2)}) async-start(), calls=%async_computation.7 | async-start | bytes 2580480 | tf_op jit(solution)/shard_map/all_gather | solution.py:83
  7.9 82.0 %all-gather.12.cloned.1.call-start = ((), (), s32[]{:S(2)}) async-start(), calls=%async_computation.8 | async-start | bytes 1081344 | tf_op jit(solution)/shard_map/all_gather | solution.py:108
  22.6 24.2 %copy-start.27 = (f32[896]{0:T(1024)}, f32[896]{0:T(1024)S(1)}, u32[]{:S(2)}) copy-start(f32[896]{0:T(1024)S(1)} %convert_element_type.166) | copy-start | bytes 10756
  23.7 22.9 %copy-start.32 = (f32[128]{0:T(128)}, f32[128]{0:T(128)S(1)}, u32[]{:S(2)}) copy-start(f32[128]{0:T(128)S(1)} %fusion.73) | copy-start | bytes 1540
  23.7 22.9 %copy-start.29 = (f32[128]{0:T(128)}, f32[128]{0:T(128)S(1)}, u32[]{:S(2)}) copy-start(f32[128]{0:T(128)S(1)} %fusion.95) | copy-start | bytes 1540
  46.5 88.4 %all-gather.14.cloned.1.call-start = ((), (), s32[]{:S(2)}) async-start(), calls=%async_computation.9 | async-start | bytes 1081344 | tf_op jit(solution)/shard_map/all_gather | solution.py:107
  47.8 149.0 %all-gather.16.cloned.1.call-start = ((), (), s32[]{:S(2)}) async-start(), calls=%async_computation.10 | async-start | bytes 2007040 | tf_op jit(solution)/shard_map/all_gather | solution.py:85
  48.4 201.0 %all-gather.18.cloned.1.call-start = ((), (), s32[]{:S(2)}) async-start(), calls=%async_computation.11 | async-start | bytes 10895360 | tf_op jit(solution)/shard_map/all_gather | solution.py:157
  48.9 288.8 %all-gather.20.cloned.1.call-start = ((), (), s32[]{:S(2)}) async-start(), calls=%async_computation.12 | async-start | bytes 10895360 | tf_op jit(solution)/shard_map/all_gather | solution.py:158
  49.5 376.7 %all-gather.22.cloned.1.call-start = ((), (), s32[]{:S(2)}) async-start(), calls=%async_computation.13 | async-start | bytes 10895360 | tf_op jit(solution)/shard_map/all_gather | solution.py:159
  50.3 558.0 %reduce-scatter.24.cloned.1.call-start = ((), (), s32[]{:S(2)}) async-start(), calls=%async_computation.21 | async-start | bytes 1081344
  181.6 15.2 %copy-start.9 = (bf16[128,896]{1,0:T(8,128)(2,1)S(1)}, bf16[128,896]{1,0:T(8,128)(2,1)}, u32[]{:S(2)}) copy-start(bf16[128,896]{1,0:T(8,128)(2,1)} %param.18) | copy-start | bytes 688132
  196.7 59.0 %copy-start.18 = (f32[128,2,7,64]{0,3,2,1:T(8,128)}, f32[128,2,7,64]{0,3,2,1:T(8,128)S(1)}, u32[]{:S(2)}) copy-start(f32[128,2,7,64]{0,3,2,1:T(8,128)S(1)} %get-tuple-element.157) | copy-start | bytes 1376260
  196.8 59.0 %copy-start.16 = (bf16[128,2,7,64]{0,3,2,1:T(8,128)(2,1)}, bf16[128,2,7,64]{0,3,2,1:T(8,128)(2,1)S(1)}, u32[]{:S(2)}) copy-start(bf16[128,2,7,64]{0,3,2,1:T(8,128)(2,1)S(1)} %convert_element_type.173) | copy-start | bytes 688132
  433.8 7.2 copy-start.12
  433.8 7.2 copy-start.11
  433.8 7.2 copy-start.2
  433.8 7.2 copy-start.4
  450.5 5.7 copy-start.1
  456.2 4.7 copy-start.26
  460.9 5.3 copy-start.20
  468.3 5.7 copy-start.1
  474.0 4.7 copy-start.26
  478.6 5.3 copy-start.20
  486.0 5.7 copy-start.1
  491.7 4.7 copy-start.26
  496.4 5.3 copy-start.20
  503.8 5.7 copy-start.1
  509.5 4.7 copy-start.26
  514.1 5.3 copy-start.20
  531.1 157.8 %reduce-scatter.22.cloned.1.call-start = ((), (), s32[]{:S(2)}) async-start(), calls=%async_computation.20 | async-start | bytes 1081344
  531.1 10.9 copy-start.7
  531.1 10.9 copy-start.17
  541.9 176.1 %reduce-scatter.14.cloned.1.call-start = ((), (), s32[]{:S(2)}) async-start(), calls=%async_computation.15 | async-start | bytes 2007040 | tf_op jit(solution)/shard_map/reduce_scatter | solution.py:272
  543.8 260.3 %reduce-scatter.16.cloned.1.call-start = ((), (), s32[]{:S(2)}) async-start(), calls=%async_computation.16 | async-start | bytes 10895360 | tf_op jit(solution)/shard_map/reduce_scatter | solution.py:278
  551.2 338.3 %reduce-scatter.18.cloned.1.call-start = ((), (), s32[]{:S(2)}) async-start(), calls=%async_computation.17 | async-start | bytes 10895360 | tf_op jit(solution)/shard_map/reduce_scatter | solution.py:281
  558.4 416.4 %reduce-scatter.20.cloned.1.call-start = ((), (), s32[]{:S(2)}) async-start(), calls=%async_computation.18 | async-start | bytes 10895360 | tf_op jit(solution)/shard_map/reduce_scatter | solution.py:284
  564.2 125.6 %copy-start.28 = (f32[896]{0:T(1024)S(1)}, f32[896]{0:T(1024)}, u32[]{:S(2)}) copy-start(f32[896]{0:T(1024)} %copy-done.27) | copy-start | bytes 10756
  564.2 125.6 %copy-start.30 = (f32[128]{0:T(128)S(1)}, f32[128]{0:T(128)}, u32[]{:S(2)}) copy-start(f32[128]{0:T(128)} %copy-done.29) | copy-start | bytes 1540
  564.2 125.6 %copy-start.10 = (bf16[128,896]{1,0:T(8,128)(2,1)S(1)}, bf16[128,896]{1,0:T(8,128)(2,1)}, u32[]{:S(2)}) copy-start(bf16[128,896]{1,0:T(8,128)(2,1)} %param.18) | copy-start | bytes 688132
  564.2 442.8 %reduce-scatter.12.cloned.1.call-start = ((), (), s32[]{:S(2)}) async-start(), calls=%async_computation.14 | async-start | bytes 2580480 | tf_op jit(solution)/shard_map/reduce_scatter | solution.py:263
  692.0 436.5 %all-reduce.17.cloned.1.call-start = ((), (), s32[]{:S(2)}) async-start(), calls=%async_computation.22 | async-start | bytes 13877248 | tf_op jit(solution)/shard_map/psum | solution.py:293
  974.8 34.1 %copy-start.5 = (f32[128,896]{1,0:T(8,128)S(1)}, f32[128,896]{1,0:T(8,128)}, u32[]{:S(2)}) copy-start(f32[128,896]{1,0:T(8,128)} %copy-done.3) | copy-start | bytes 1376260
  974.9 228.1 %all-gather.24.cloned.1.call-start = ((), (), s32[]{:S(2)}) async-start(), calls=%async_computation.19 | async-start | bytes 17031168 | tf_op jit(solution)/shard_map/all_gather | solution.py:12
  1009.0 6.0 copy-start.15
  1014.7 75.6 %copy-start.33 = (f32[128]{0:T(128)S(1)}, f32[128]{0:T(128)}, u32[]{:S(2)}) copy-start(f32[128]{0:T(128)} %copy-done.32) | copy-start | bytes 1540
  1128.5 6.1 copy-start.14
  (27 other events, 69.7 us)
Sparse Core Ops, SparseCore 0:
  9.7 33.8 all-gather.9
  46.6 43.2 all-gather.11
  92.8 42.0 all-gather.13
  136.4 25.5 all-gather.15
  163.5 85.8 all-gather.17
  250.8 86.8 all-gather.19
  339.4 86.8 all-gather.21
  531.2 77.0 reduce-scatter.23
  612.2 76.6 reduce-scatter.21
  691.7 26.2 reduce-scatter.13
  720.5 83.4 reduce-scatter.15
  806.6 82.8 reduce-scatter.17
  891.9 82.8 reduce-scatter.19
  977.8 29.0 reduce-scatter.11
  1010.8 117.6 all-reduce.16
  1130.9 72.0 all-gather.23
